TPU v7x, 256 devices: a whole 4x4x8 slice. The times are simulated.
256 devices in a mesh: kz: 4 (over y_hi, core), pw: 64 (over x, y_lo, z).
Axes of the slice: x: 4, y: 4 (y_hi: 2, y_lo: 2; y = y_hi * 2 + y_lo), z: 8, core: 2. Of those that a mesh axis runs over, the one named last changes fastest.
Arguments:
- waves: bfloat16 [16, 1, 16384, 2, 256], P('kz', None, 'pw'), may hold values from -1.25 to 1.25
- pw_map: int32 [1, 16384], P(None, 'pw'), may hold values from 0 to 16383, each once within a row
Outputs:
- correlation_plus: float32 [16, 1, 2, 256, 256], P('kz', None, None, 'pw')
- correlation_minus: float32 [16, 1, 2, 256, 256], P('kz', None, None, 'pw')
Inputs may be any that keep to these rules, and one draw needn't show every extreme that they name: Each row of pw_map is a permutation of the 16384 plane waves.
All inputs are finite; a program needn't handle non-finite values.
Results may differ from a plain program's by a relative error of at most 0.0003.
Values may be sent and summed in bfloat16 or wider, within the bound.
No kernel may reach another device: no remote copies, remote signals or barrier semaphores. Data moves between devices by JAX's collectives and lax.ppermute only.
A program may use at most 128 MiB of HBM per device.

v0:
```python
import jax
import jax.numpy as jnp
from jax import lax
from jax.sharding import PartitionSpec as P


def shifted(block, axis, distance):
    devices = range(lax.axis_size(axis))
    route = [((i - distance) % len(devices), i) for i in devices]
    return lax.ppermute(block, axis, route)


def make_term(left, right, count):
    prods = jnp.einsum("kcgpn,kcgqm->nkcpqm", left, right, preferred_element_type=jnp.float32)
    real_part = prods[:, :, :, 0, 0] + prods[:, :, :, 1, 1]
    imag_part = prods[:, :, :, 0, 1] - prods[:, :, :, 1, 0]
    return jnp.stack([real_part, imag_part], axis=3).reshape(count, -1)


def body(waves, pw_map):
    kz_dev, cols, rows, _, bands = waves.shape
    band_rows = bands // lax.axis_size("pw")
    kz_pos = lax.axis_index("kz")
    last_pos = lax.axis_size("kz") - 1
    arriving = shifted(waves[0], "kz", -1)
    source = jnp.where(kz_pos == last_pos, arriving, waves[0])
    piece = lax.all_gather(source, "pw", axis=1, tiled=True)
    count = piece.shape[1]
    inside = (pw_map >= 0) & (pw_map < count)
    index = jnp.clip(pw_map, 0, count - 1)
    values = jnp.take_along_axis(piece.reshape(cols, count, 2 * bands), index[:, :, None], axis=1)
    moved = jnp.where(inside[:, :, None], values, jnp.zeros_like(values))
    moved = moved.reshape(cols, rows, 2, bands)
    boundary = jnp.where(kz_pos == last_pos, moved, arriving)
    upper = jnp.concatenate([waves[1:], boundary[None]], axis=0)
    summed = lax.psum_scatter(
        make_term(waves, upper, band_rows * lax.axis_size("pw")),
        "pw",
        scatter_dimension=0,
        tiled=True,
    )
    correlation_plus = summed.reshape(band_rows, kz_dev, cols, 2, bands).transpose(1, 2, 3, 0, 4)
    leaving = shifted(waves[kz_dev - 1], "kz", 1)
    opening = jnp.where(kz_pos == 0, moved, waves[0])
    left_side = jnp.concatenate([opening[None], waves[1:]], axis=0)
    lower = jnp.concatenate([leaving[None], waves[:-1]], axis=0)
    summed_back = lax.psum_scatter(
        make_term(left_side, lower, band_rows * lax.axis_size("pw")),
        "pw",
        scatter_dimension=0,
        tiled=True,
    )
    correlation_minus = summed_back.reshape(band_rows, kz_dev, cols, 2, bands).transpose(
        1, 2, 3, 0, 4
    )
    return (correlation_plus, correlation_minus)


def solution(mesh):
    placed = (P("kz", None, "pw", None, None), P(None, "pw"))
    return jax.shard_map(
        body,
        mesh=mesh,
        in_specs=placed,
        out_specs=(P("kz", None, None, "pw", None), P("kz", None, None, "pw", None)),
        check_vma=False,
    )
```

profile of v0, /device:TPU:16, one launch (start us, length us, event | category | flops | bytes accessed | tf_op | source)
XLA Modules:
  0.0 1021.0 jit_solution(3574576932487633641)
XLA Ops:
  7.2 0.0 copy-start
  7.2 0.0 copy-start.5
  7.2 0.0 all-gather.2.cloned.1.call-start
  7.2 1.5 fusion.15
  8.7 0.2 copy.67
  8.9 0.0 copy-start.1
  8.9 0.1 collective-permute-start
  9.0 3.9 collective-permute-done
  12.9 0.0 copy-start.3
  12.9 0.8 broadcast_select_fusion
  13.6 0.0 all-gather.2.cloned.1.call-update
  13.7 0.0 all-reduce.5.cloned.1.call-start
  13.7 0.9 copy.70
  14.6 3.2 collective-permute-start.1
  17.9 0.0 copy-done.5
  17.9 0.0 copy-done
  17.9 0.9 fusion.16
  18.8 0.0 copy-done.1
  18.9 0.0 copy-done.3
  18.9 0.6 copy.66
  19.5 0.6 copy.71
  20.1 334.8 %all-gather.2.cloned.1.call-done = bf16[1,16384,2,256]{1,3,2,0:T(8,128)(2,1)} async-done(((bf16[1,256,2,256]{1,3,2,0:T(8,128)(2,1)}), bf16[1,16384,2,256]{1,3,2,0:T(8,128)(2,1)}) %all-gather.2.cloned.1.call-update) | async-done | bytes 16777232 | tf_op jit(solution)/shard_map/all_gather | solution.py:27
  354.9 22.4 %copy.38 = bf16[16384,512]{1,0:T(8,128)(2,1)} copy(bf16[16384,512]{0,1:T(8,128)(2,1)} %bitcast.84) | data formatting | bytes 33554432 | tf_op jit(solution)/shard_map/reshape | solution.py:31
  377.2 0.0 copy-start.2
  377.2 9.2 gather_fusion
  386.4 0.1 copy.39
  386.6 0.0 copy-done.2
  386.6 0.0 collective-permute-done.1
  386.6 1.7 convolution_bitcast_fusion
  388.3 0.1 fusion
  388.5 0.0 copy-start.4
  388.5 0.1 fusion.2
  388.6 0.8 copy-done.4
  389.5 0.7 convolution_bitcast_fusion.1
  390.2 0.1 fusion.3
  390.3 0.1 fusion.5
  390.5 0.1 pad_maximum_fusion.1
  390.6 1.5 copy.52
  392.1 0.1 pad_maximum_fusion
  392.2 1.5 copy.43
  393.7 0.0 copy-start.6
  393.7 0.0 all-reduce.5.cloned.1.call-update
  393.8 0.6 copy-done.6
  394.4 0.6 dynamic-slice
  395.6 614.5 %all-reduce.5.cloned.1.call-done = (f32[256,2048]{0,1:T(8,128)}, f32[256,2048]{0,1:T(8,128)}) async-done(((f32[256,2048]{0,1:T(8,128)}, f32[256,2048]{0,1:T(8,128)}), (f32[256,2048]{0,1:T(8,128)}, f32[256,2048]{0,1:T(8,128)})) %all-reduce.5.cloned.1.call-update) | async-done | bytes 4194320
  1010.1 2.1 constant_dynamic-slice_fusion
  1012.2 0.9 copy.44
  1013.2 0.9 copy.53
  (7 shorter events, 0.1 us)
Async XLA Ops:
  7.2 10.8 %copy-start = (bf16[4,1,256,2,256]{4,3,2,1,0:T(2,128)(2,1)S(1)}, bf16[4,1,256,2,256]{4,3,2,1,0:T(2,128)(2,1)}, u32[]{:S(2)}) copy-start(bf16[4,1,256,2,256]{4,3,2,1,0:T(2,128)(2,1)} %param.2) | copy-start | bytes 3145732
  7.2 10.7 %copy-start.5 = (s32[1,256]{1,0:T(1,128)S(1)}, s32[1,256]{1,0:T(1,128)}, u32[]{:S(2)}) copy-start(s32[1,256]{1,0:T(1,128)} %param.3) | copy-start | bytes 3076
  7.2 347.7 %all-gather.2.cloned.1.call-start = ((), (), s32[]{:S(2)}) async-start(), calls=%async_computation | async-start | bytes 17039360 | tf_op jit(solution)/shard_map/all_gather | solution.py:27
  8.9 10.0 copy-start.1
  8.9 4.0 collective-permute-start
  12.9 6.0 copy-start.3
  13.7 996.4 %all-reduce.5.cloned.1.call-start = ((), (), s32[]{:S(2)}) async-start(), calls=%async_computation.1 | async-start | bytes 8388608
  14.6 372.0 %collective-permute-start.1 = (bf16[1,256,2,256]{1,3,2,0:T(8,128)(2,1)}, bf16[1,256,2,256]{1,3,2,0:T(8,128)(2,1)}, u32[]{:S(2)}, u32[]{:S(2)}) collective-permute-start(bf16[1,256,2,256]{1,3,2,0:T(8,128)(2,1)} %bitcast.20), channel_id=1, source_target_pairs={{192,0},{0,64},{64,128},{128,192},{193,1},{1,65},{65,129},{129,193... | collective-permute-start | bytes 786440 | tf_op jit(solution)/shard_map/ppermute | solution.py:10
  377.2 9.3 copy-start.2
  388.5 1.0 copy-start.4
  393.7 0.7 copy-start.6
Sparse Core Ops, SparseCore 0:
  13.8 341.0 all-gather.1
  393.9 616.1 all-reduce.4
where the time goes:
time: 1020 us
  waiting for transfers between devices  953 us (93%)
  local copies, waits for them, and re-layouts  45.3 us (4%)
  between operations  14.9 us (1%)
    unnamed x3, waiting for transfers between devices  614 us
    all_gather x1, waiting for transfers between devices, body(): piece = lax.all_gather(source, 'pw', axis=1, tiled=True)  335 us
    reshape x1, local copies, waits for them, and re-layouts, body(): piece.reshape(cols, count, 2 * bands)  22.4 us
  transfers between devices with their start and end apart: 4, of which 3 were waited for; matrix products, arithmetic and copies ran while one was open for 3% of the time, Pallas kernels for 0%

commit v1 on v0

--- a/solution.py
+++ b/solution.py
@@ -24,7 +24,10 @@
     last_pos = lax.axis_size("kz") - 1
     arriving = shifted(waves[0], "kz", -1)
     source = jnp.where(kz_pos == last_pos, arriving, waves[0])
-    piece = lax.all_gather(source, "pw", axis=1, tiled=True)
+    size = lax.axis_size("pw")
+    blocks = jnp.stack([source for _ in range(size)])
+    blocks = lax.all_to_all(blocks, "pw", split_axis=0, concat_axis=0)
+    piece = jnp.concatenate(blocks, axis=1)
     count = piece.shape[1]
     inside = (pw_map >= 0) & (pw_map < count)
     index = jnp.clip(pw_map, 0, count - 1)

time: 1020 us -> 1100 us (1.078)
  waiting for transfers between devices: 953 us -> 1020 us
  starting transfers between devices: 3.4 us -> 16.1 us
    all_to_all x0 -> x1, waiting for transfers between devices: none -> 365 us  [body(): blocks = lax.all_to_all(blocks, 'pw', split_axis=0, concat_axis=0)]
    all_gather x1 -> x0, waiting for transfers between devices: 335 us -> none  [body(): piece = lax.all_gather(source, 'pw', axis=1, tiled=True)]
    unnamed x3 -> x2, waiting for transfers between devices: 614 us -> 649 us
    reshape x1 -> x0, local copies, waits for them, and re-layouts: 22.4 us -> none  [body(): piece.reshape(cols, count, 2 * bands)]
    unnamed x20 -> x21, local copies, waits for them, and re-layouts: 6.42 us -> 24 us
    all_to_all x0 -> x1, starting transfers between devices: none -> 13.7 us  [body(): blocks = lax.all_to_all(blocks, 'pw', split_axis=0, concat_axis=0)]
where the time goes in v1:
time: 1100 us
  waiting for transfers between devices  1020 us (93%)
  local copies, waits for them, and re-layouts  51 us (5%)
  starting transfers between devices  16.1 us (1%)
  between operations  14.9 us (1%)
    unnamed x2, waiting for transfers between devices  649 us
    all_to_all x1, waiting for transfers between devices, body(): blocks = lax.all_to_all(blocks, 'pw', split_axis=0, concat_axis=0)  365 us
    unnamed x21, local copies, waits for them, and re-layouts  24 us
  transfers between devices with their start and end apart: 4, of which 3 were waited for; matrix products, arithmetic and copies ran while one was open for 3% of the time, Pallas kernels for 0%

profile of v1, /device:TPU:16, one launch (start us, length us, event | category | flops | bytes accessed | tf_op | source)
XLA Modules:
  0.0 1103.3 jit_solution(9062805444167812322)
XLA Ops:
  7.2 1.4 fusion.15
  8.6 0.2 copy.67
  8.7 0.0 copy-start.1
  8.8 0.1 collective-permute-start
  8.8 3.9 collective-permute-done
  12.7 0.0 copy-start.3
  12.7 0.7 copy-done.3
  13.5 0.2 copy.38
  13.6 0.0 copy-done.1
  13.7 10.3 stack.6
  23.9 0.0 copy-start.5
  23.9 0.0 copy-start
  23.9 13.7 %all-to-all-start = ((bf16[64,1,256,2,256]{4,3,2,1,0:T(2,128)(2,1)}), bf16[64,1,256,2,256]{4,3,2,1,0:T(2,128)(2,1)}, u32[]{:S(2)}, u32[]{:S(2)}) async-start(bf16[64,1,256,2,256]{4,3,2,1,0:T(2,128)(2,1)} %stack.6), calls=%async_computation | async-start | bytes 33554432 | tf_op jit(solution)/shard_map/all_to_all | solution.py:29
  37.7 0.0 all-reduce.5.cloned.1.call-start
  37.7 0.9 copy.70
  38.6 2.3 collective-permute-start.1
  40.9 0.0 copy-done.5
  41.0 0.0 copy-done
  41.0 0.9 fusion.16
  41.9 0.6 copy.66
  42.5 0.6 copy.71
  43.1 364.7 %all-to-all-done = bf16[64,1,256,2,256]{4,3,2,1,0:T(2,128)(2,1)} async-done(((bf16[64,1,256,2,256]{4,3,2,1,0:T(2,128)(2,1)}), bf16[64,1,256,2,256]{4,3,2,1,0:T(2,128)(2,1)}, u32[]{:S(2)}, u32[]{:S(2)}) %all-to-all-start) | async-done | bytes 16777248 | tf_op jit(solution)/shard_map/all_to_all | solution.py:29
  407.8 16.9 %copy.74 = bf16[2048,8,2,256]{3,1,2,0:T(8,128)(2,1)} copy(bf16[2048,8,2,256]{3,2,1,0:T(2,128)(2,1)} %bitcast.53) | data formatting | bytes 33554432
  424.7 0.0 copy-start.2
  424.7 9.2 gather_fusion
  433.9 0.1 copy.39
  434.1 0.0 copy-done.2
  434.1 0.0 collective-permute-done.1
  434.1 1.7 convolution_bitcast_fusion
  435.8 0.1 fusion
  436.0 0.0 copy-start.4
  436.0 0.1 fusion.2
  436.1 0.8 copy-done.4
  437.0 0.7 convolution_bitcast_fusion.1
  437.7 0.1 fusion.3
  437.8 0.1 fusion.5
  438.0 0.1 pad_maximum_fusion.1
  438.1 1.5 copy.52
  439.6 0.1 pad_maximum_fusion
  439.7 1.5 copy.43
  441.2 0.0 copy-start.6
  441.2 0.0 all-reduce.5.cloned.1.call-update
  441.3 0.6 copy-done.6
  441.9 0.6 dynamic-slice
  443.1 649.2 %all-reduce.5.cloned.1.call-done = (f32[256,2048]{0,1:T(8,128)}, f32[256,2048]{0,1:T(8,128)}) async-done(((f32[256,2048]{0,1:T(8,128)}, f32[256,2048]{0,1:T(8,128)}), (f32[256,2048]{0,1:T(8,128)}, f32[256,2048]{0,1:T(8,128)})) %all-reduce.5.cloned.1.call-update) | async-done | bytes 4194320
  1092.4 2.1 constant_dynamic-slice_fusion
  1094.5 0.9 copy.44
  1095.5 0.9 copy.53
  (8 shorter events, 0.2 us)
Async XLA Ops:
  8.7 4.9 copy-start.1
  8.8 4.0 collective-permute-start
  12.7 0.7 copy-start.3
  23.9 17.0 %copy-start.5 = (s32[1,256]{1,0:T(1,128)S(1)}, s32[1,256]{1,0:T(1,128)}, u32[]{:S(2)}) copy-start(s32[1,256]{1,0:T(1,128)} %param.3) | copy-start | bytes 3076
  23.9 17.0 %copy-start = (bf16[4,1,256,2,256]{4,3,2,1,0:T(2,128)(2,1)S(1)}, bf16[4,1,256,2,256]{4,3,2,1,0:T(2,128)(2,1)}, u32[]{:S(2)}) copy-start(bf16[4,1,256,2,256]{4,3,2,1,0:T(2,128)(2,1)} %param.2) | copy-start | bytes 3145732
  23.9 383.8 %all-to-all-start = ((bf16[64,1,256,2,256]{4,3,2,1,0:T(2,128)(2,1)}), bf16[64,1,256,2,256]{4,3,2,1,0:T(2,128)(2,1)}, u32[]{:S(2)}, u32[]{:S(2)}) async-start(bf16[64,1,256,2,256]{4,3,2,1,0:T(2,128)(2,1)} %stack.6), calls=%async_computation | async-start | bytes 33554432 | tf_op jit(solution)/shard_map/all_to_all | solution.py:29
  37.7 1054.7 %all-reduce.5.cloned.1.call-start = ((), (), s32[]{:S(2)}) async-start(), calls=%async_computation.1 | async-start | bytes 8388608
  38.6 395.5 %collective-permute-start.1 = (bf16[1,256,2,256]{1,3,2,0:T(8,128)(2,1)}, bf16[1,256,2,256]{1,3,2,0:T(8,128)(2,1)}, u32[]{:S(2)}, u32[]{:S(2)}) collective-permute-start(bf16[1,256,2,256]{1,3,2,0:T(8,128)(2,1)} %bitcast.20), channel_id=1, source_target_pairs={{192,0},{0,64},{64,128},{128,192},{193,1},{1,65},{65,129},{129,193... | collective-permute-start | bytes 786440 | tf_op jit(solution)/shard_map/ppermute | solution.py:10
  424.7 9.3 copy-start.2
  436.0 1.0 copy-start.4
  441.2 0.7 copy-start.6
Sparse Core Ops, SparseCore 0:
  441.4 650.9 all-reduce.4
